TPU v7x, 32 devices: a whole 2x2x4 slice. The times are simulated.
32 devices in a mesh: row: 8 (over y, x, core), col: 4 (over z).
Axes of the slice: x: 2, y: 2, z: 4, core: 2. Of those that a mesh axis runs over, the one named last changes fastest.
Arguments:
- precision: float32 [16384, 16384], P('row', 'col'), may hold values from -0.3 to 4, as said below
- samples: bfloat16 [1024, 16384], P(None, 'col'), may hold values from -6 to 6
- step_size: float32 [1], replicated, may hold values from 0.5 to 1
- threshold: float32 [1], replicated, may hold values from 0.1 to 0.3
Outputs:
- updated: float32 [16384, 16384], P('row', 'col')
Inputs may be any that keep to these rules, and one draw needn't show every extreme that they name: precision is symmetric; its diagonal entries lie between 1 and 4.
All inputs are finite; a program needn't handle non-finite values.
Results may differ from a plain program's by a relative error of at most 0.0056.
Values may be sent and summed in bfloat16 or wider, within the bound.
A program may use at most 192 MiB of HBM per device.

v0:
```python
import jax
import jax.numpy as jnp
from jax import lax
from jax.sharding import PartitionSpec as P


def broadcast(block, axis, holder):
    block = jnp.where(lax.axis_index(axis) == holder, block, jnp.zeros_like(block))
    return lax.psum(block, axis)


def per_device(precision, samples, step_size, threshold):
    rows_tile, cols_tile = precision.shape
    sample_count = samples.shape[0]
    col_count = lax.axis_size("col")
    rounded = precision.astype(jnp.bfloat16)
    sample_part = samples
    projected = lax.psum_scatter(
        lax.dot_general(
            sample_part, rounded, (((1,), (1,)), ((), ())), preferred_element_type=jnp.float32
        ),
        "col",
        scatter_dimension=0,
        tiled=True,
    ).astype(jnp.bfloat16)
    sample_part = samples
    cross_tile = (
        lax.dot_general(
            lax.all_gather(projected, "col", axis=0, tiled=True),
            sample_part,
            (((0,), (0,)), ((), ())),
            preferred_element_type=jnp.float32,
        )
        / sample_count
    )
    row_index = lax.axis_index("row")
    col_index = lax.axis_index("col")
    row_ratio = lax.axis_size("row") // col_count
    full_panel = lax.all_gather(projected, "row", axis=1, tiled=True)
    dealt = lax.all_to_all(full_panel, "col", split_axis=1, concat_axis=0, tiled=True)
    own_columns = lax.dynamic_slice_in_dim(samples, row_index % row_ratio * rows_tile, rows_tile, 1)
    own_columns = broadcast(own_columns, "col", row_index // row_ratio)
    mirrored = (
        lax.dot_general(
            own_columns, dealt, (((0,), (0,)), ((), ())), preferred_element_type=jnp.float32
        )
        / sample_count
    )
    symmetric = 0.5 * (cross_tile + mirrored)
    global_row = row_index * rows_tile + jnp.arange(rows_tile, dtype=jnp.int32)
    global_col = col_index * cols_tile + jnp.arange(cols_tile, dtype=jnp.int32)
    on_diagonal = global_row[:, None] == global_col[None, :]
    gradient = symmetric - jnp.where(on_diagonal, 1.0 / jnp.where(on_diagonal, precision, 1.0), 0.0)
    stepped = precision - step_size[0] * gradient
    shrunk = jnp.sign(stepped) * jnp.maximum(jnp.abs(stepped) - step_size[0] * threshold[0], 0.0)
    return jnp.where(on_diagonal, stepped, shrunk)


def solution(mesh):
    in_specs = (P("row", "col"), P(None, "col"), P(), P())
    out_specs = P("row", "col")
    return jax.shard_map(
        per_device, mesh=mesh, in_specs=in_specs, out_specs=out_specs, check_vma=False
    )
```

profile of v0, /device:TPU:5, one launch (start us, length us, event | category | flops | bytes accessed | tf_op | source)
XLA Modules:
  0.0 703.5 jit_solution(8990483182471119099)
XLA Ops:
  6.5 0.0 reduce-scatter.2.cloned.1.call-start
  6.5 25.2 %fusion.4 = f32[1024,2048]{1,0:T(8,128)} fusion(bf16[1024,4096]{1,0:T(8,128)(2,1)} %param.5, f32[2048,4096]{1,0:T(8,128)} %param.4), kind=kOutput, calls=%fused_computation.7 | convolution fusion | flops 17188257792 | bytes 50331648 | tf_op jit(solution)/shard_map/dot_general | solution.py:19
  31.8 0.0 reduce-scatter.2.cloned.1.call-update
  31.8 0.0 all-gather.5.cloned.1.call-start
  31.8 145.6 %reduce-scatter.2.cloned.1.call-done = f32[256,2048]{1,0:T(8,128)} async-done(((f32[1024,2048]{1,0:T(8,128)}), f32[256,2048]{1,0:T(8,128)}) %reduce-scatter.2.cloned.1.call-update) | async-done | bytes 2097168 | tf_op jit(solution)/shard_map/reduce_scatter | solution.py:18
  177.4 2.7 convert_element_type.7
  180.2 0.0 all-gather.5.cloned.1.call-update
  180.2 55.5 %all-gather.5.cloned.1.call-done = bf16[256,16384]{1,0:T(8,128)(2,1)} async-done(((bf16[256,2048]{1,0:T(8,128)(2,1)}), bf16[256,16384]{1,0:T(8,128)(2,1)}) %all-gather.5.cloned.1.call-update) | async-done | bytes 8388624 | tf_op jit(solution)/shard_map/all_gather | solution.py:39
  235.7 7.7 %copy.8 = bf16[32,4,8,4096]{3,2,0,1:T(8,128)(2,1)} copy(bf16[32,4,8,4096]{3,2,1,0:T(8,128)(2,1)} %bitcast.18) | data formatting | bytes 16777216 | tf_op jit(solution)/shard_map/all_to_all | solution.py:40
  243.4 5.7 all-to-all-start
  249.1 0.0 all-gather.3.cloned.1.call-start
  249.1 0.7 all-gather.3.cloned.1.call-update
  249.8 0.0 all-reduce.2.cloned.1.call-start
  249.9 5.5 dynamic-slice_select_fusion
  255.4 0.0 all-reduce.2.cloned.1.call-update
  256.7 143.7 %all-gather.3.cloned.1.call-done = bf16[1024,2048]{1,0:T(8,128)(2,1)} async-done(((bf16[256,2048]{1,0:T(8,128)(2,1)}), bf16[1024,2048]{1,0:T(8,128)(2,1)}) %all-gather.3.cloned.1.call-update) | async-done | bytes 4194320 | tf_op jit(solution)/shard_map/all_gather | solution.py:29
  400.4 25.5 %fusion.6 = f32[2048,4096]{1,0:T(8,128)} fusion(bf16[1024,2048]{1,0:T(8,128)(2,1)} %all-gather.3.cloned.1.call-done, bf16[1024,4096]{1,0:T(8,128)(2,1)} %param.5), kind=kOutput, calls=%fused_computation.13 | convolution fusion | flops 17179869184 | bytes 46137344 | tf_op jit(solution)/shard_map/dot_general | solution.py:28
  425.9 219.5 %all-reduce.2.cloned.1.call-done = bf16[1024,2048]{1,0:T(8,128)(2,1)} async-done(((bf16[1024,2048]{1,0:T(8,128)(2,1)}), bf16[1024,2048]{1,0:T(8,128)(2,1)}) %all-reduce.2.cloned.1.call-update) | async-done | bytes 4194320 | tf_op jit(solution)/shard_map/psum | solution.py:9
  645.4 0.0 all-to-all-done
  645.4 51.6 %compare_select_fusion = f32[2048,4096]{1,0:T(8,128)} fusion(f32[2048,4096]{1,0:T(8,128)} %param.4, f32[2048,4096]{1,0:T(8,128)} %fusion.6, bf16[1024,2048]{1,0:T(8,128)(2,1)} %all-reduce.2.cloned.1.call-done, bf16[1024,4096]{1,0:T(8,128)(2,1)} %bitcast.2, f32[]{:T(128)S(6)} %mul.34, f32[]{:T(128)} %bitcast.14, s32[4096]{0:T(1024)S(1)} %iota_add_fusion, ...), kind=kOutput, calls=%fused_computation | convolution fusion | flops 17305698304 | bytes 113270792 | tf_op jit(solution)/shard_map/dot_general | solution.py:44
  (2 shorter events, 0.0 us)
Async XLA Ops:
  6.5 170.9 %reduce-scatter.2.cloned.1.call-start = ((), (), s32[]{:S(2)}) async-start(), calls=%async_computation.2 | async-start | bytes 10485760 | tf_op jit(solution)/shard_map/reduce_scatter | solution.py:18
  31.8 203.9 %all-gather.5.cloned.1.call-start = ((), (), s32[]{:S(2)}) async-start(), calls=%async_computation.5 | async-start | bytes 9437184 | tf_op jit(solution)/shard_map/all_gather | solution.py:39
  243.4 402.0 %all-to-all-start = ((bf16[256,4,4096]{2,0,1:T(8,128)(2,1)}), bf16[256,4,4096]{2,0,1:T(8,128)(2,1)}, u32[]{:S(2)}, u32[]{:S(2)}) async-start(bf16[256,4,4096]{2,0,1:T(8,128)(2,1)} %bitcast.17), calls=%async_computation.1 | async-start | bytes 16777216 | tf_op jit(solution)/shard_map/all_to_all | solution.py:40
  249.1 151.3 %all-gather.3.cloned.1.call-start = ((), (), s32[]{:S(2)}) async-start(), calls=%async_computation.3 | async-start | bytes 5242880 | tf_op jit(solution)/shard_map/all_gather | solution.py:29
  249.8 395.6 %all-reduce.2.cloned.1.call-start = ((), (), s32[]{:S(2)}) async-start(), calls=%async_computation.4 | async-start | bytes 8388608 | tf_op jit(solution)/shard_map/psum | solution.py:9
Sparse Core Ops, SparseCore 0:
  31.9 145.4 reduce-scatter.1
  180.3 55.3 all-gather.4
  251.5 148.8 all-gather.2
  402.6 242.7 all-reduce.1
where the time goes:
time: 705 us; the launch traced here: 704 us
  waiting for transfers between devices  565 us (80%)
  matrix products  102 us (14%)
  between operations  14.5 us (2%)
  other arithmetic  8.2 us (1%)
  local copies, waits for them, and re-layouts  7.72 us (1%)
    psum x1, waiting for transfers between devices, broadcast(): return lax.psum(block, axis)  219 us
    reduce_scatter x1, waiting for transfers between devices, per_device(): lax.psum_scatter(lax.dot_general(sample_part, rounded, (((1,), (1,)), (()...  146 us
    all_gather x1, waiting for transfers between devices, per_device(): lax.all_gather(projected, 'col', axis=0, tiled=True)  144 us
    all_gather x1, waiting for transfers between devices, per_device(): full_panel = lax.all_gather(projected, 'row', axis=1, tiled=True)  55.5 us
    dot_general x1, matrix products, per_device(): lax.dot_general(own_columns, dealt, (((0,), (0,)), ((), ())), preferred_e...  51.6 us
    dot_general x1, matrix products, per_device(): lax.dot_general(lax.all_gather(projected, 'col', axis=0, tiled=True), sam...  25.5 us
    dot_general x1, matrix products, per_device(): lax.dot_general(sample_part, rounded, (((1,), (1,)), ((), ())), preferred...  25.2 us
  transfers between devices with their start and end apart: 5, of which 4 were waited for; matrix products, arithmetic and copies ran while one was open for 4% of the time, Pallas kernels for 0%

commit v1 on v0

v1 whole, which is shorter than its diff:
```python
import functools

import jax
import jax.numpy as jnp
from jax import lax
from jax.experimental import pallas as pl
from jax.experimental.pallas import tpu as pltpu
from jax.sharding import PartitionSpec as P

MESH = pl.DeviceIdType.MESH
PARTS = 2


def ring_place(group, groups):
    place = jnp.int32(0)
    for spot in range(groups):
        place = jnp.where(group == (spot ^ (spot >> 1)), spot, place)
    return place


def ring_group(place, groups):
    group = jnp.int32(0)
    for spot in range(groups):
        group = jnp.where(place == spot, spot ^ (spot >> 1), group)
    return group


def spread_kernel(
    row_count,
    col_count,
    block_ref,
    own_ref,
    samples_ref,
    left_ref,
    right_ref,
    gather_send,
    gather_recv,
    ring_send,
    ring_recv,
    core_send,
    core_recv,
    local_sem,
    step_sem,
):
    row, col = lax.axis_index("row"), lax.axis_index("col")
    ratio = row_count // col_count
    groups = col_count
    group, core = row // ratio, row % ratio
    depth, rows_tile = block_ref.shape
    total = samples_ref.shape[0]
    place = ring_place(group, groups)
    behind = lax.rem(place - ring_place(col, groups) + groups, groups)
    ahead = lax.rem(groups - behind, groups)
    next_row = ring_group(lax.rem(place + 1, groups), groups) * ratio + core
    last_row = ring_group(lax.rem(place + groups - 1, groups), groups) * ratio + core
    is_root = behind == 0

    peers = [(row, lax.rem(col + step, col_count)) for step in range(1, col_count)]
    peers += [(next_row, col), (last_row, col)]
    peers += [(group * ratio + lax.rem(core + step, ratio), col) for step in range(1, ratio)]
    barrier = pltpu.get_barrier_semaphore()
    for peer in peers:
        pl.semaphore_signal(barrier, inc=1, device_id=peer, device_id_type=MESH)
    pl.semaphore_wait(barrier, len(peers))

    part = depth // PARTS
    columns = pl.ds(pl.multiple_of(core * rows_tile, 128), rows_tile)

    def rows_of(step, piece, start):
        holder = lax.rem(col + step, col_count)
        return pl.ds(pl.multiple_of(start + holder * depth + piece * part, 16), part)

    def gather(step, piece):
        mine = rows_of(0, piece, 0)
        return pltpu.make_async_remote_copy(
            src_ref=block_ref.at[pl.ds(piece * part, part), :],
            dst_ref=left_ref.at[mine, :],
            send_sem=gather_send.at[step, piece],
            recv_sem=gather_recv.at[step, piece],
            device_id=(row, lax.rem(col - step + col_count, col_count)),
            device_id_type=MESH,
        )

    def arrival(step, piece):
        theirs = left_ref.at[rows_of(step, piece, 0), :]
        return pltpu.make_async_remote_copy(
            src_ref=theirs,
            dst_ref=theirs,
            send_sem=gather_send.at[step, piece],
            recv_sem=gather_recv.at[step, piece],
            device_id=(row, lax.rem(col - step + col_count, col_count)),
            device_id_type=MESH,
        )

    def ring(step, piece):
        held = right_ref.at[rows_of(step, piece, total), columns]
        return pltpu.make_async_remote_copy(
            src_ref=held,
            dst_ref=held,
            send_sem=ring_send.at[step, piece],
            recv_sem=ring_recv.at[step, piece],
            device_id=(next_row if (step + piece) % 2 == 0 else last_row, col),
            device_id_type=MESH,
        )

    def across(step, piece, hop, incoming):
        from_core = lax.rem(core + ratio - hop, ratio) if incoming else core
        there = pl.ds(pl.multiple_of(from_core * rows_tile, 128), rows_tile)
        held = right_ref.at[rows_of(step, piece, total), there]
        return pltpu.make_async_remote_copy(
            src_ref=held,
            dst_ref=held,
            send_sem=core_send.at[hop, step, piece],
            recv_sem=core_recv.at[hop, step, piece],
            device_id=(group * ratio + lax.rem(core + hop, ratio), col),
            device_id_type=MESH,
        )

    for piece in range(PARTS):
        for step in range(1, col_count):
            gather(step, piece).start()
    own_rows = pl.ds(pl.multiple_of(col * depth, 16), depth)
    local = [
        pltpu.make_async_copy(block_ref, left_ref.at[own_rows, :], local_sem.at[0]),
        pltpu.make_async_copy(own_ref, left_ref.at[pl.ds(total, total), :], local_sem.at[1]),
        pltpu.make_async_copy(samples_ref, right_ref.at[pl.ds(0, total), :], local_sem.at[2]),
    ]
    for copy in local:
        copy.start()

    for step in range(col_count):
        for piece in range(PARTS):
            travelled = behind if (step + piece) % 2 == 0 else ahead

            @pl.when(is_root)
            def _():
                if step == 0:
                    source = block_ref.at[pl.ds(piece * part, part), :]
                else:
                    arrival(step, piece).wait_recv()
                    source = left_ref.at[rows_of(step, piece, 0), :]
                copy = pltpu.make_async_copy(
                    source, right_ref.at[rows_of(step, piece, total), columns], step_sem.at[0]
                )
                copy.start()
                copy.wait()

            @pl.when(jnp.logical_not(is_root))
            def _():
                ring(step, piece).wait_recv()

            @pl.when(travelled < groups - 1)
            def _():
                ring(step, piece).start()

            for hop in range(1, ratio):
                across(step, piece, hop, False).start()

    for step in range(col_count):
        for piece in range(PARTS):
            travelled = behind if (step + piece) % 2 == 0 else ahead

            @pl.when(travelled < groups - 1)
            def _():
                ring(step, piece).wait_send()

            if step:
                @pl.when(jnp.logical_not(is_root))
                def _():
                    arrival(step, piece).wait_recv()

                gather(step, piece).wait_send()
            for hop in range(1, ratio):
                across(step, piece, hop, False).wait_send()
                across(step, piece, hop, True).wait_recv()
    for copy in local:
        copy.wait()


def spread(block, own, samples, row_count, col_count):
    total, cols_tile = samples.shape
    rows_tile = own.shape[1]
    ratio = row_count // col_count
    anywhere = pl.BlockSpec(memory_space=pl.ANY)
    pair = pltpu.SemaphoreType.DMA((col_count, PARTS))
    triple = pltpu.SemaphoreType.DMA((ratio, col_count, PARTS))
    return pl.pallas_call(
        functools.partial(spread_kernel, row_count, col_count),
        out_shape=(
            jax.ShapeDtypeStruct((2 * total, rows_tile), jnp.bfloat16),
            jax.ShapeDtypeStruct((2 * total, cols_tile), jnp.bfloat16),
        ),
        in_specs=[anywhere] * 3,
        out_specs=(anywhere, anywhere),
        scratch_shapes=[
            pair,
            pair,
            pair,
            pair,
            triple,
            triple,
            pltpu.SemaphoreType.DMA((3,)),
            pltpu.SemaphoreType.DMA((1,)),
        ],
        compiler_params=pltpu.CompilerParams(collective_id=0, has_side_effects=True),
    )(block, own, samples)


def per_device(precision, samples, step_size, threshold):
    rows_tile, cols_tile = precision.shape
    sample_count = samples.shape[0]
    row_count, col_count = lax.axis_size("row"), lax.axis_size("col")
    row_index, col_index = lax.axis_index("row"), lax.axis_index("col")
    share = sample_count // row_count
    piece = lax.dynamic_slice_in_dim(samples, row_index * share, share, 0)
    panel = lax.all_gather(piece, "col", axis=1, tiled=True)
    own_samples = lax.all_to_all(panel, "row", split_axis=1, concat_axis=0, tiled=True)

    depth = sample_count // col_count
    rounded = precision.astype(jnp.bfloat16)
    partial = lax.dot_general(
        samples, rounded, (((1,), (1,)), ((), ())), preferred_element_type=jnp.float32
    ).astype(jnp.bfloat16)
    terms = lax.all_to_all(
        partial.reshape(col_count, depth, rows_tile), "col", split_axis=0, concat_axis=0
    )
    block = jnp.sum(terms.astype(jnp.float32), axis=0).astype(jnp.bfloat16)

    left, right = spread(block, own_samples, samples, row_count, col_count)
    symmetric = lax.dot_general(
        left, right, (((0,), (0,)), ((), ())), preferred_element_type=jnp.float32
    ) * (0.5 / sample_count)
    global_row = row_index * rows_tile + jnp.arange(rows_tile, dtype=jnp.int32)
    global_col = col_index * cols_tile + jnp.arange(cols_tile, dtype=jnp.int32)
    on_diagonal = global_row[:, None] == global_col[None, :]
    gradient = symmetric - jnp.where(on_diagonal, 1.0 / jnp.where(on_diagonal, precision, 1.0), 0.0)
    stepped = precision - step_size[0] * gradient
    shrunk = jnp.sign(stepped) * jnp.maximum(jnp.abs(stepped) - step_size[0] * threshold[0], 0.0)
    return jnp.where(on_diagonal, stepped, shrunk)


def solution(mesh):
    in_specs = (P("row", "col"), P(None, "col"), P(), P())
    out_specs = P("row", "col")
    return jax.shard_map(
        per_device, mesh=mesh, in_specs=in_specs, out_specs=out_specs, check_vma=False
    )
```

time: 705 us -> 903 us (1.28)
  Pallas kernels: 0 us -> 599 us
  waiting for transfers between devices: 565 us -> 177 us
  matrix products: 102 us -> 90.7 us
    pallas_call x0 -> x1, Pallas kernels: none -> 599 us  [spread(): pl.pallas_call(functools.partial(spread_kernel, row_count, col_count), ou...]
    psum x1 -> x0, waiting for transfers between devices: 219 us -> none  [broadcast(): return lax.psum(block, axis)]
    reduce_scatter x1 -> x0, waiting for transfers between devices: 146 us -> none  [per_device(): lax.psum_scatter(lax.dot_general(sample_part, rounded, (((1,), (1,)), (()...]
    all_gather x2 -> x1, waiting for transfers between devices: 199 us -> 122 us  [per_device(): panel = lax.all_gather(piece, 'col', axis=1, tiled=True)]
    all_to_all x1 -> x2, waiting for transfers between devices: 0.01 us -> 55.3 us  [the longest x1 39.8 us: per_device(): lax.all_to_all(panel, 'row', split_axis=1, concat_axis=0, tiled=True)]
    dot_general x3 -> x2, matrix products: 102 us -> 90.7 us  [the longest x1 65.8 us: per_device(): lax.dot_general(left, right, (((0,), (0,)), ((), ())), preferred_element_...]
  transfers between devices with their start and end apart: 5 -> 3, of which waited for: 4 -> 3; matrix products, arithmetic and copies ran while one was open for 4% -> 4% of each run, Pallas kernels for 0% -> 0%
where the time goes in v1:
time: 903 us
  Pallas kernels  599 us (66%)
  waiting for transfers between devices  177 us (20%)
  matrix products  90.7 us (10%)
  between operations  14.7 us (2%)
  starting transfers between devices  10 us (1%)
    pallas_call x1, Pallas kernels, spread(): pl.pallas_call(functools.partial(spread_kernel, row_count, col_count), ou...  599 us
    all_gather x1, waiting for transfers between devices, per_device(): panel = lax.all_gather(piece, 'col', axis=1, tiled=True)  122 us
    dot_general x1, matrix products, per_device(): lax.dot_general(left, right, (((0,), (0,)), ((), ())), preferred_element_...  65.8 us
    all_to_all x1, waiting for transfers between devices, per_device(): lax.all_to_all(panel, 'row', split_axis=1, concat_axis=0, tiled=True)  39.8 us
    dot_general x1, matrix products, per_device(): lax.dot_general(samples, rounded, (((1,), (1,)), ((), ())), preferred_ele...  24.9 us
  transfers between devices with their start and end apart: 3, of which 3 were waited for; matrix products, arithmetic and copies ran while one was open for 4% of the time, Pallas kernels for 0%

profile of v1, /device:TPU:5, one launch (start us, length us, event | category | flops | bytes accessed | tf_op | source)
XLA Modules:
  0.0 902.9 jit_solution(13306307334893581134)
XLA Ops:
  6.5 0.0 all-gather.2.cloned.1.call-start
  6.5 2.3 constant_dynamic-slice_fusion
  8.8 0.0 all-gather.2.cloned.1.call-update
  8.9 24.9 %fusion.6 = bf16[1024,2048]{1,0:T(8,128)(2,1)} fusion(bf16[1024,4096]{1,0:T(8,128)(2,1)} %samples_ref.1, f32[2048,4096]{1,0:T(8,128)} %param.4), kind=kOutput, calls=%fused_computation.10 | convolution fusion | flops 17190354944 | bytes 46137344 | tf_op jit(solution)/shard_map/dot_general | solution.py:221
  33.7 4.9 all-to-all-start
  38.6 121.6 %all-gather.2.cloned.1.call-done = bf16[128,16384]{1,0:T(8,128)(2,1)} async-done(((bf16[128,4096]{1,0:T(8,128)(2,1)}), bf16[128,16384]{1,0:T(8,128)(2,1)}) %all-gather.2.cloned.1.call-update) | async-done | bytes 4194320 | tf_op jit(solution)/shard_map/all_gather | solution.py:216
  160.2 4.8 copy.8
  164.9 15.5 %all-to-all-done = bf16[4,256,2048]{2,1,0:T(8,128)(2,1)} async-done(((bf16[4,256,2048]{2,1,0:T(8,128)(2,1)}), bf16[4,256,2048]{2,1,0:T(8,128)(2,1)}, u32[]{:S(2)}, u32[]{:S(2)}) %all-to-all-start) | async-done | bytes 4194336 | tf_op jit(solution)/shard_map/all_to_all | solution.py:224
  180.5 5.2 all-to-all-start.1
  186.9 4.3 reduce_sum.12.block_ref
  191.2 39.8 %all-to-all-done.1 = bf16[128,8,2048]{2,0,1:T(8,128)(2,1)} async-done(((bf16[128,8,2048]{2,0,1:T(8,128)(2,1)}), bf16[128,8,2048]{2,0,1:T(8,128)(2,1)}, u32[]{:S(2)}, u32[]{:S(2)}) %all-to-all-start.1) | async-done | bytes 4194336 | tf_op jit(solution)/shard_map/all_to_all | solution.py:217
  231.0 599.3 %shard_map.46 = (bf16[2048,2048]{1,0:T(8,128)(2,1)}, bf16[2048,4096]{1,0:T(8,128)(2,1)}) custom-call(bf16[256,2048]{1,0:T(8,128)(2,1)} %reduce_sum.12.block_ref, bf16[1024,2048]{1,0:T(8,128)(2,1)} %bitcast.3.own_ref, bf16[1024,4096]{1,0:T(8,128)(2,1)} %samples_ref.1), custom_call_target="tpu_custom_call" | custom-call | tf_op jit(solution)/shard_map/pallas_call | solution.py:187
  830.3 65.8 %compare_select_fusion = f32[2048,4096]{1,0:T(8,128)} fusion(f32[2048,4096]{1,0:T(8,128)} %param.4, bf16[2048,2048]{1,0:T(8,128)(2,1)} %get-tuple-element.7, bf16[2048,4096]{1,0:T(8,128)(2,1)} %get-tuple-element.8, f32[]{:T(128)S(6)} %mul.34, f32[]{:T(128)} %bitcast.13, s32[4096]{0:T(1024)S(1)} %iota_add_fusion, s32[2048]{0:T(1024)S(1)} %iota_add_fusion.1), kind=kOutput, calls=%fused_computation | convolution fusion | flops 34477178880 | bytes 92299272 | tf_op jit(solution)/shard_map/dot_general | solution.py:230
  (2 shorter events, 0.0 us)
Async XLA Ops:
  6.5 153.7 %all-gather.2.cloned.1.call-start = ((), (), s32[]{:S(2)}) async-start(), calls=%async_computation.2 | async-start | bytes 5242880 | tf_op jit(solution)/shard_map/all_gather | solution.py:216
  33.7 146.7 %all-to-all-start = ((bf16[4,256,2048]{2,1,0:T(8,128)(2,1)}), bf16[4,256,2048]{2,1,0:T(8,128)(2,1)}, u32[]{:S(2)}, u32[]{:S(2)}) async-start(bf16[4,256,2048]{2,1,0:T(8,128)(2,1)} %bitcast.18), calls=%async_computation | async-start | bytes 8388608 | tf_op jit(solution)/shard_map/all_to_all | solution.py:224
  180.5 50.5 %all-to-all-start.1 = ((bf16[128,8,2048]{2,0,1:T(8,128)(2,1)}), bf16[128,8,2048]{2,0,1:T(8,128)(2,1)}, u32[]{:S(2)}, u32[]{:S(2)}) async-start(bf16[128,8,2048]{2,0,1:T(8,128)(2,1)} %bitcast.16), calls=%async_computation.1 | async-start | bytes 8388608 | tf_op jit(solution)/shard_map/all_to_all | solution.py:217
Sparse Core Ops, SparseCore 0:
  9.0 151.1 all-gather.1

commit v2 on v1

--- a/solution.py
+++ b/solution.py
@@ -29,7 +29,7 @@
     row_count,
     col_count,
     block_ref,
-    own_ref,
+    panel_ref,
     samples_ref,
     left_ref,
     right_ref,
@@ -39,8 +39,15 @@
     ring_recv,
     core_send,
     core_recv,
-    local_sem,
+    deal_send,
+    deal_recv,
+    load_sem,
+    store_sem,
     step_sem,
+    block_held,
+    own_held,
+    samples_held,
+    part_held,
 ):
     row, col = lax.axis_index("row"), lax.axis_index("col")
     ratio = row_count // col_count
@@ -56,8 +63,7 @@
     is_root = behind == 0
 
     peers = [(row, lax.rem(col + step, col_count)) for step in range(1, col_count)]
-    peers += [(next_row, col), (last_row, col)]
-    peers += [(group * ratio + lax.rem(core + step, ratio), col) for step in range(1, ratio)]
+    peers += [(lax.rem(row + step, row_count), col) for step in range(1, row_count)]
     barrier = pltpu.get_barrier_semaphore()
     for peer in peers:
         pl.semaphore_signal(barrier, inc=1, device_id=peer, device_id_type=MESH)
@@ -116,17 +122,54 @@
             device_id_type=MESH,
         )
 
+    share = panel_ref.shape[0]
+
+    def deal(step):
+        taker = lax.rem(row - step + row_count, row_count)
+        return pltpu.make_async_remote_copy(
+            src_ref=panel_ref.at[:, pl.ds(pl.multiple_of(taker * rows_tile, 128), rows_tile)],
+            dst_ref=left_ref.at[pl.ds(pl.multiple_of(total + row * share, 16), share), :],
+            send_sem=deal_send.at[step],
+            recv_sem=deal_recv.at[step],
+            device_id=(taker, col),
+            device_id_type=MESH,
+        )
+
+    def dealt(step):
+        giver = lax.rem(row + step, row_count)
+        theirs = left_ref.at[pl.ds(pl.multiple_of(total + giver * share, 16), share), :]
+        return pltpu.make_async_remote_copy(
+            src_ref=theirs,
+            dst_ref=theirs,
+            send_sem=deal_send.at[step],
+            recv_sem=deal_recv.at[step],
+            device_id=(giver, col),
+            device_id_type=MESH,
+        )
+
     for piece in range(PARTS):
         for step in range(1, col_count):
             gather(step, piece).start()
+    for step in range(1, row_count):
+        deal(step).start()
     own_rows = pl.ds(pl.multiple_of(col * depth, 16), depth)
-    local = [
-        pltpu.make_async_copy(block_ref, left_ref.at[own_rows, :], local_sem.at[0]),
-        pltpu.make_async_copy(own_ref, left_ref.at[pl.ds(total, total), :], local_sem.at[1]),
-        pltpu.make_async_copy(samples_ref, right_ref.at[pl.ds(0, total), :], local_sem.at[2]),
-    ]
-    for copy in local:
+    mine = panel_ref.at[:, pl.ds(pl.multiple_of(row * rows_tile, 128), rows_tile)]
+    kept_rows = pl.ds(pl.multiple_of(total + row * share, 16), share)
+    loads, stores = [], []
+    for index, (source, held, target) in enumerate(
+        (
+            (block_ref, block_held, left_ref.at[own_rows, :]),
+            (mine, own_held, left_ref.at[kept_rows, :]),
+            (samples_ref, samples_held, right_ref.at[pl.ds(0, total), :]),
+        )
+    ):
+        loads.append(pltpu.make_async_copy(source, held, load_sem.at[index]))
+        stores.append(pltpu.make_async_copy(held, target, store_sem.at[index]))
+    for copy in loads:
         copy.start()
+    for load, store in zip(loads, stores):
+        load.wait()
+        store.start()
 
     for step in range(col_count):
         for piece in range(PARTS):
@@ -135,15 +178,20 @@
             @pl.when(is_root)
             def _():
                 if step == 0:
-                    source = block_ref.at[pl.ds(piece * part, part), :]
+                    source = block_held.at[pl.ds(piece * part, part), :]
                 else:
                     arrival(step, piece).wait_recv()
-                    source = left_ref.at[rows_of(step, piece, 0), :]
-                copy = pltpu.make_async_copy(
-                    source, right_ref.at[rows_of(step, piece, total), columns], step_sem.at[0]
+                    source = part_held
+                    load = pltpu.make_async_copy(
+                        left_ref.at[rows_of(step, piece, 0), :], part_held, step_sem.at[0]
+                    )
+                    load.start()
+                    load.wait()
+                store = pltpu.make_async_copy(
+                    source, right_ref.at[rows_of(step, piece, total), columns], step_sem.at[1]
                 )
-                copy.start()
-                copy.wait()
+                store.start()
+                store.wait()
 
             @pl.when(jnp.logical_not(is_root))
             def _():
@@ -173,13 +221,17 @@
             for hop in range(1, ratio):
                 across(step, piece, hop, False).wait_send()
                 across(step, piece, hop, True).wait_recv()
-    for copy in local:
-        copy.wait()
-
-
-def spread(block, own, samples, row_count, col_count):
+    for step in range(1, row_count):
+        deal(step).wait_send()
+        dealt(step).wait_recv()
+    for store in stores:
+        store.wait()
+
+
+def spread(block, panel, samples, row_count, col_count):
     total, cols_tile = samples.shape
-    rows_tile = own.shape[1]
+    depth, rows_tile = block.shape
+    share = panel.shape[0]
     ratio = row_count // col_count
     anywhere = pl.BlockSpec(memory_space=pl.ANY)
     pair = pltpu.SemaphoreType.DMA((col_count, PARTS))
@@ -199,11 +251,20 @@
             pair,
             triple,
             triple,
+            pltpu.SemaphoreType.DMA((row_count,)),
+            pltpu.SemaphoreType.DMA((row_count,)),
             pltpu.SemaphoreType.DMA((3,)),
-            pltpu.SemaphoreType.DMA((1,)),
+            pltpu.SemaphoreType.DMA((3,)),
+            pltpu.SemaphoreType.DMA((2,)),
+            pltpu.VMEM((depth, rows_tile), jnp.bfloat16),
+            pltpu.VMEM((share, rows_tile), jnp.bfloat16),
+            pltpu.VMEM((total, cols_tile), jnp.bfloat16),
+            pltpu.VMEM((depth // PARTS, rows_tile), jnp.bfloat16),
         ],
-        compiler_params=pltpu.CompilerParams(collective_id=0, has_side_effects=True),
-    )(block, own, samples)
+        compiler_params=pltpu.CompilerParams(
+            collective_id=0, has_side_effects=True, vmem_limit_bytes=40 * 2**20
+        ),
+    )(block, panel, samples)
 
 
 def per_device(precision, samples, step_size, threshold):
@@ -214,7 +275,6 @@
     share = sample_count // row_count
     piece = lax.dynamic_slice_in_dim(samples, row_index * share, share, 0)
     panel = lax.all_gather(piece, "col", axis=1, tiled=True)
-    own_samples = lax.all_to_all(panel, "row", split_axis=1, concat_axis=0, tiled=True)
 
     depth = sample_count // col_count
     rounded = precision.astype(jnp.bfloat16)
@@ -226,7 +286,7 @@
     )
     block = jnp.sum(terms.astype(jnp.float32), axis=0).astype(jnp.bfloat16)
 
-    left, right = spread(block, own_samples, samples, row_count, col_count)
+    left, right = spread(block, panel, samples, row_count, col_count)
     symmetric = lax.dot_general(
         left, right, (((0,), (0,)), ((), ())), preferred_element_type=jnp.float32
     ) * (0.5 / sample_count)

time: 903 us -> 490 us (0.54)
  Pallas kernels: 599 us -> 212 us
  waiting for transfers between devices: 177 us -> 156 us
    pallas_call x1, Pallas kernels: 599 us -> 212 us  [spread(): pl.pallas_call(functools.partial(spread_kernel, row_count, col_count), ou...]
    all_to_all x1, waiting for transfers between devices: 15.5 us -> 156 us  [per_device(): lax.all_to_all(partial.reshape(col_count, depth, rows_tile), 'col', split...]
    all_gather x1, waiting for transfers between devices: 122 us -> 0.02 us  [per_device(): panel = lax.all_gather(piece, 'col', axis=1, tiled=True)]
    all_to_all x1 -> x0, waiting for transfers between devices: 39.8 us -> none  [per_device(): lax.all_to_all(panel, 'row', split_axis=1, concat_axis=0, tiled=True)]
  transfers between devices with their start and end apart: 3 -> 2, of which waited for: 3 -> 1; matrix products, arithmetic and copies ran while one was open for 4% -> 1% of each run, Pallas kernels for 0% -> 0%
where the time goes in v2:
time: 490 us; the launch traced here: 489 us
  Pallas kernels  212 us (43%)
  waiting for transfers between devices  156 us (32%)
  matrix products  90.5 us (18%)
  between operations  14.8 us (3%)
  local copies, waits for them, and re-layouts  7.76 us (2%)
    pallas_call x1, Pallas kernels, spread(): pl.pallas_call(functools.partial(spread_kernel, row_count, col_count), ou...  212 us
    all_to_all x1, waiting for transfers between devices, per_device(): lax.all_to_all(partial.reshape(col_count, depth, rows_tile), 'col', split...  156 us
    dot_general x1, matrix products, per_device(): lax.dot_general(left, right, (((0,), (0,)), ((), ())), preferred_element_...  65.6 us
    dot_general x1, matrix products, per_device(): lax.dot_general(samples, rounded, (((1,), (1,)), ((), ())), preferred_ele...  24.9 us
  transfers between devices with their start and end apart: 2, of which 1 were waited for; matrix products, arithmetic and copies ran while one was open for 1% of the time, Pallas kernels for 0%

profile of v2, /device:TPU:5, one launch (start us, length us, event | category | flops | bytes accessed | tf_op | source)
XLA Modules:
  0.0 489.1 jit_solution(18105431310938479391)
XLA Ops:
  6.5 24.9 %fusion.6 = bf16[1024,2048]{1,0:T(8,128)(2,1)} fusion(bf16[1024,4096]{1,0:T(8,128)(2,1)} %samples_ref.1, f32[2048,4096]{1,0:T(8,128)} %param.4), kind=kOutput, calls=%fused_computation.9 | convolution fusion | flops 17190354944 | bytes 46137344 | tf_op jit(solution)/shard_map/dot_general | solution.py:281
  31.4 4.8 all-to-all-start
  36.3 0.0 all-gather.2.cloned.1.call-start
  36.3 2.4 constant_dynamic-slice_fusion
  38.7 0.0 all-gather.2.cloned.1.call-update
  40.0 156.3 %all-to-all-done = bf16[4,256,2048]{2,1,0:T(8,128)(2,1)} async-done(((bf16[4,256,2048]{2,1,0:T(8,128)(2,1)}), bf16[4,256,2048]{2,1,0:T(8,128)(2,1)}, u32[]{:S(2)}, u32[]{:S(2)}) %all-to-all-start) | async-done | bytes 4194336 | tf_op jit(solution)/shard_map/all_to_all | solution.py:284
  196.3 3.1 reduce_sum.12.block_ref
  199.4 0.0 all-gather.2.cloned.1.call-done.panel_ref
  199.4 0.0 copy-start
  199.4 2.2 copy-done
  201.6 211.7 %shard_map.46 = (bf16[2048,2048]{1,0:T(8,128)(2,1)S(1)}, bf16[2048,4096]{1,0:T(8,128)(2,1)}) custom-call(bf16[256,2048]{1,0:T(8,128)(2,1)S(1)} %reduce_sum.12.block_ref, bf16[128,16384]{1,0:T(8,128)(2,1)S(1)} %copy-done, bf16[1024,4096]{1,0:T(8,128)(2,1)} %samples_ref.1), custom_call_target="tpu_custom_call" | custom-call | tf_op jit(solution)/shard_map/pallas_call | solution.py:239
  413.4 0.0 copy-start.1
  413.4 3.2 copy-done.1
  416.6 65.6 %compare_select_fusion = f32[2048,4096]{1,0:T(8,128)} fusion(f32[2048,4096]{1,0:T(8,128)} %param.4, bf16[2048,2048]{1,0:T(8,128)(2,1)} %copy-done.1, bf16[2048,4096]{1,0:T(8,128)(2,1)} %get-tuple-element.8, f32[]{:T(128)S(6)} %mul.34, f32[]{:T(128)} %bitcast.6, s32[4096]{0:T(1024)S(1)} %iota_add_fusion, s32[2048]{0:T(1024)S(1)} %iota_add_fusion.1), kind=kOutput, calls=%fused_computation | convolution fusion | flops 34477178880 | bytes 92299272 | tf_op jit(solution)/shard_map/dot_general | solution.py:290
  (2 shorter events, 0.0 us)
Async XLA Ops:
  31.4 164.9 %all-to-all-start = ((bf16[4,256,2048]{2,1,0:T(8,128)(2,1)}), bf16[4,256,2048]{2,1,0:T(8,128)(2,1)}, u32[]{:S(2)}, u32[]{:S(2)}) async-start(bf16[4,256,2048]{2,1,0:T(8,128)(2,1)} %bitcast.9), calls=%async_computation | async-start | bytes 8388608 | tf_op jit(solution)/shard_map/all_to_all | solution.py:284
  36.3 163.2 %all-gather.2.cloned.1.call-start = ((), (), s32[]{:S(2)}) async-start(), calls=%async_computation.1 | async-start | bytes 5242880 | tf_op jit(solution)/shard_map/all_gather | solution.py:277
  199.4 2.2 copy-start
  413.4 3.2 copy-start.1
Sparse Core Ops, SparseCore 0:
  38.8 148.5 all-gather.1
